TPU v7x, 1024 devices: a whole 8x8x8 slice. The times are simulated.
1024 devices in a mesh: dp: 16 (over z_hi, x), section: 8 (over z_lo, core), tensor: 8 (over y).
Axes of the slice: x: 8, y: 8, z: 8 (z_hi: 2, z_lo: 4; z = z_hi * 4 + z_lo), core: 2. Of those that a mesh axis runs over, the one named last changes fastest.
Arguments:
- section_inputs: bfloat16 [8, 2, 4096, 8192], P('section', None, 'dp', 'tensor'), may hold values from -6 to 6
- out_grad: bfloat16 [2, 4096, 8192], P(None, 'dp', 'tensor'), may hold values from -6 to 6
- layer_gain: float32 [8, 8192], P('section', 'tensor'), may hold values from 0.6 to 1.2
- init_factor: float32 [8, 8192, 128], P('section', 'tensor'), may hold values from -0.0625 to 0.0625
Outputs:
- sent_grads: bfloat16 [8, 2, 4096, 8192], P('section', None, 'dp', 'tensor')
- residue_out: float32 [8, 4096, 8192], P('section', 'dp', 'tensor')
- gain_grad: float32 [8, 8192], P('section', 'tensor')
All inputs are finite; a program needn't handle non-finite values.
Results may differ from a plain program's by a relative error of at most 0.003.
Values sent between devices are 32-bit elements; how exact they have to be, the bound alone decides.
No kernel may reach another device: no remote copies, remote signals or barrier semaphores. Data moves between devices by JAX's collectives and lax.ppermute only.
A program may use at most 32 MiB of HBM per device.

v0:
```python
import jax
import jax.numpy as jnp
from jax import lax
from jax.sharding import PartitionSpec as P


def shifted(array, axis, by):
    size = lax.axis_size(axis)
    pairs = [(i, i + by) for i in range(size) if 0 <= i + by < size]
    return lax.ppermute(array, axis, pairs)


def outer_product(left, right):
    return lax.dot_general(
        left,
        right,
        (((1,), (1,)), ((), ())),
        preferred_element_type=jnp.float32,
        precision=lax.Precision.HIGHEST,
    )


def inner_rows(left, right):
    return lax.dot_general(
        left,
        right,
        (((0,), (0,)), ((), ())),
        preferred_element_type=jnp.float32,
        precision=lax.Precision.HIGHEST,
    )


def body(section_inputs, out_grad, layer_gain, init_factor):
    section_count = lax.axis_size("section")
    section_index = lax.axis_index("section")
    micro_count = section_inputs.shape[1]
    row_count = section_inputs.shape[2]
    width_local = section_inputs.shape[3]
    rank_size = init_factor.shape[2]
    saved_all = section_inputs[0]
    gain_row = layer_gain[0]
    basis = init_factor[0]
    is_last = section_index == section_count - 1
    steps_total = micro_count * section_count

    def locate(counter):
        micro_index = counter // section_count
        active = section_count - 1 - counter % section_count == section_index
        return (jnp.clip(micro_index, 0, micro_count - 1), active)

    def front_work(operands):
        recv_p, recv_q, residue, micro_index = operands
        incoming = outer_product(recv_p, recv_q)
        given = lax.dynamic_index_in_dim(out_grad, micro_index, 0, keepdims=False).astype(
            jnp.float32
        )
        upstream = jnp.where(is_last, given, incoming)
        saved = lax.dynamic_index_in_dim(saved_all, micro_index, 0, keepdims=False).astype(
            jnp.float32
        )
        soft = jnp.tanh(saved)
        local = upstream * gain_row * (1.0 + soft * soft)
        gain_term = jnp.sum(upstream * (2.0 * saved - soft), axis=0)
        merged = local + residue
        partial_value = jnp.dot(
            merged, basis, preferred_element_type=jnp.float32, precision=lax.Precision.HIGHEST
        )
        return (merged, partial_value, gain_term, local.astype(jnp.bfloat16))

    def front_skip(operands):
        return (
            jnp.zeros((row_count, width_local), jnp.float32),
            jnp.zeros((row_count, rank_size), jnp.float32),
            jnp.zeros((width_local,), jnp.float32),
            jnp.zeros((row_count, width_local), jnp.bfloat16),
        )

    def back_work(operands):
        merged, proj, residue = operands
        gram = inner_rows(proj, proj)
        lower = jnp.linalg.cholesky(gram)
        ortho = lax.linalg.triangular_solve(
            lower, proj, left_side=False, lower=True, transpose_a=True
        )
        factor_q = inner_rows(merged, ortho)
        return (ortho, factor_q, merged - outer_product(ortho, factor_q))

    def back_skip(operands):
        merged, proj, residue = operands
        return (
            jnp.zeros((row_count, rank_size), jnp.float32),
            jnp.zeros((width_local, rank_size), jnp.float32),
            residue,
        )

    def advance(counter, carry):
        recv_p, recv_q, residue, gain_total, sent = carry
        micro_index, active = locate(counter)
        merged, partial_value, gain_term, local_bf = lax.cond(
            active, front_work, front_skip, (recv_p, recv_q, residue, micro_index)
        )
        proj = lax.psum(partial_value, "tensor")
        packed_p, packed_q, residue = lax.cond(
            active, back_work, back_skip, (merged, proj, residue)
        )
        recv_p, recv_q = shifted((packed_p, packed_q), "section", -1)
        previous = lax.dynamic_index_in_dim(sent, micro_index, 0, keepdims=False)
        sent = lax.dynamic_update_index_in_dim(
            sent, jnp.where(active, local_bf, previous), micro_index, 0
        )
        return (recv_p, recv_q, residue, gain_total + gain_term, sent)

    start = (
        jnp.zeros((row_count, rank_size), jnp.float32),
        jnp.zeros((width_local, rank_size), jnp.float32),
        jnp.zeros((row_count, width_local), jnp.float32),
        jnp.zeros((width_local,), jnp.float32),
        jnp.zeros((micro_count, row_count, width_local), jnp.bfloat16),
    )
    recv_p, recv_q, residue, gain_total, sent = lax.fori_loop(0, steps_total, advance, start)
    summed = lax.psum(gain_total, "dp")
    token_total = micro_count * row_count * lax.axis_size("dp")
    gain_grad = summed * (1.0 / jnp.sqrt(jnp.float32(token_total)))
    return (sent[None], residue[None], gain_grad[None])


def solution(mesh):
    placed = (
        P("section", None, "dp", "tensor"),
        P(None, "dp", "tensor"),
        P("section", "tensor"),
        P("section", "tensor", None),
    )
    return jax.shard_map(
        body,
        mesh=mesh,
        in_specs=placed,
        out_specs=(
            P("section", None, "dp", "tensor"),
            P("section", "dp", "tensor"),
            P("section", "tensor"),
        ),
        check_vma=False,
    )
```

profile of v0, /device:TPU:176, one launch (start us, length us, event | category | flops | bytes accessed | tf_op | source)
XLA Modules:
  0.0 2089.8 jit_solution(1618832745445017370)
XLA Ops:
  9.4 2018.0 %while.27 = (s32[]{:T(128)}, f32[256,128]{0,1:T(8,128)S(1)}, f32[1024,128]{0,1:T(8,128)S(1)}, f32[256,1024]{1,0:T(8,128)S(1)}, f32[1024]{0:T(1024)S(1)}, /*index...) while((s32[]{:T(128)}, f32[256,128]{0,1:T(8,128)S(1)}, ...), condition=%wide.region_9.10_spmd.clone, body=%wide.region_0.9_spmd.clone.sunk | while | flops 1715389568 | bytes 18634944 | solution.py:120
  11.3 96.2 %all-reduce.2.cloned.1.call-done = f32[256,128]{1,0:T(8,128)} async-done(((f32[256,128]{1,0:T(8,128)}), f32[256,128]{1,0:T(8,128)}) %all-reduce.2.cloned.1.call-update) | async-done | bytes 131088 | tf_op jit(solution)/shard_map/while/body/eval_jaxpr/psum | solution.py:102
  113.0 2.2 collective-permute-start
  115.2 4.1 collective-permute-done
  121.1 105.5 %all-reduce.2.cloned.1.call-done = f32[256,128]{1,0:T(8,128)} async-done(((f32[256,128]{1,0:T(8,128)}), f32[256,128]{1,0:T(8,128)}) %all-reduce.2.cloned.1.call-update) | async-done | bytes 131088 | tf_op jit(solution)/shard_map/while/body/eval_jaxpr/psum | solution.py:102
  232.1 2.2 collective-permute-start
  234.3 4.1 collective-permute-done
  240.2 115.9 %all-reduce.2.cloned.1.call-done = f32[256,128]{1,0:T(8,128)} async-done(((f32[256,128]{1,0:T(8,128)}), f32[256,128]{1,0:T(8,128)}) %all-reduce.2.cloned.1.call-update) | async-done | bytes 131088 | tf_op jit(solution)/shard_map/while/body/eval_jaxpr/psum | solution.py:102
  361.7 2.2 collective-permute-start
  363.9 4.1 collective-permute-done
  369.8 108.2 %all-reduce.2.cloned.1.call-done = f32[256,128]{1,0:T(8,128)} async-done(((f32[256,128]{1,0:T(8,128)}), f32[256,128]{1,0:T(8,128)}) %all-reduce.2.cloned.1.call-update) | async-done | bytes 131088 | tf_op jit(solution)/shard_map/while/body/eval_jaxpr/psum | solution.py:102
  483.5 2.2 collective-permute-start
  485.7 4.1 collective-permute-done
  491.7 116.4 %all-reduce.2.cloned.1.call-done = f32[256,128]{1,0:T(8,128)} async-done(((f32[256,128]{1,0:T(8,128)}), f32[256,128]{1,0:T(8,128)}) %all-reduce.2.cloned.1.call-update) | async-done | bytes 131088 | tf_op jit(solution)/shard_map/while/body/eval_jaxpr/psum | solution.py:102
  613.6 2.2 collective-permute-start
  615.8 24.6 %collective-permute-done = f32[256,128]{0,1:T(8,128)S(1)} collective-permute-done((f32[256,128]{0,1:T(8,128)}, f32[256,128]{0,1:T(8,128)S(1)}, u32[]{:S(2)}, u32[]{:S(2)}) %collective-permute-start) | collective-permute-done | bytes 131104 | tf_op jit(solution)/shard_map/while/body/eval_jaxpr/ppermute | solution.py:10
  640.5 5.8 conditional.6
  640.5 3.6 fusion.8
  644.1 2.2 fusion.14
  647.0 83.5 %all-reduce.2.cloned.1.call-done = f32[256,128]{1,0:T(8,128)} async-done(((f32[256,128]{1,0:T(8,128)}), f32[256,128]{1,0:T(8,128)}) %all-reduce.2.cloned.1.call-update) | async-done | bytes 131088 | tf_op jit(solution)/shard_map/while/body/eval_jaxpr/psum | solution.py:102
  730.5 30.6 %conditional.7 = (f32[256,128]{0,1:T(8,128)}, f32[1024,128]{0,1:T(8,128)}, f32[256,1024]{1,0:T(8,128)S(1)}) conditional(s32[]{:T(128)} %convert_element_type.52, f32[256,1024]{1,0:T(8,128)S(1)} %get-tuple-element.547, (f32[256,128]{1,0:T(8,128)}, f32[256,1024]{1,0:T(8,128)}) %tuple.78), branch_computations={%region_5.5_spmd, %region_6.8_spmd} | conditional | flops 906379392 | bytes 6030390 | solution.py:103
  732.0 11.7 cholesky.2
  745.1 9.8 custom-call.5
  755.9 2.8 fusion.16
  758.7 2.5 convolution_subtract_fusion
  767.1 4.4 collective-permute-done
  773.3 87.8 %all-reduce.2.cloned.1.call-done = f32[256,128]{1,0:T(8,128)} async-done(((f32[256,128]{1,0:T(8,128)}), f32[256,128]{1,0:T(8,128)}) %all-reduce.2.cloned.1.call-update) | async-done | bytes 131088 | tf_op jit(solution)/shard_map/while/body/eval_jaxpr/psum | solution.py:102
  862.6 25.6 %collective-permute-start.1 = (f32[1024,128]{0,1:T(8,128)}, f32[1024,128]{0,1:T(8,128)S(1)}, u32[]{:S(2)}, u32[]{:S(2)}) collective-permute-start(f32[1024,128]{0,1:T(8,128)} %get-tuple-element.508), channel_id=1, source_target_pairs={{8,0},{16,8},{24,16},{32,24},{40,32},{48,40},{56,48},{9,1},{17,9},... | collective-permute-start | bytes 1572872 | tf_op jit(solution)/shard_map/while/body/eval_jaxpr/ppermute | solution.py:10
  892.3 4.4 collective-permute-done
  898.5 86.0 %all-reduce.2.cloned.1.call-done = f32[256,128]{1,0:T(8,128)} async-done(((f32[256,128]{1,0:T(8,128)}), f32[256,128]{1,0:T(8,128)}) %all-reduce.2.cloned.1.call-update) | async-done | bytes 131088 | tf_op jit(solution)/shard_map/while/body/eval_jaxpr/psum | solution.py:102
  990.0 31.3 %collective-permute-start = (f32[256,128]{0,1:T(8,128)}, f32[256,128]{0,1:T(8,128)S(1)}, u32[]{:S(2)}, u32[]{:S(2)}) collective-permute-start(f32[256,128]{0,1:T(8,128)} %get-tuple-element.507), channel_id=1, source_target_pairs={{8,0},{16,8},{24,16},{32,24},{40,32},{48,40},{56,48},{9,1},{17,9},... | collective-permute-start | bytes 393224 | tf_op jit(solution)/shard_map/while/body/eval_jaxpr/ppermute | solution.py:10
  1021.3 2.8 collective-permute-done
  1026.0 85.2 %all-reduce.2.cloned.1.call-done = f32[256,128]{1,0:T(8,128)} async-done(((f32[256,128]{1,0:T(8,128)}), f32[256,128]{1,0:T(8,128)}) %all-reduce.2.cloned.1.call-update) | async-done | bytes 131088 | tf_op jit(solution)/shard_map/while/body/eval_jaxpr/psum | solution.py:102
  1116.7 2.2 collective-permute-start
  1118.9 4.1 collective-permute-done
  1124.8 105.5 %all-reduce.2.cloned.1.call-done = f32[256,128]{1,0:T(8,128)} async-done(((f32[256,128]{1,0:T(8,128)}), f32[256,128]{1,0:T(8,128)}) %all-reduce.2.cloned.1.call-update) | async-done | bytes 131088 | tf_op jit(solution)/shard_map/while/body/eval_jaxpr/psum | solution.py:102
  1235.8 2.2 collective-permute-start
  1238.0 4.1 collective-permute-done
  1243.9 115.9 %all-reduce.2.cloned.1.call-done = f32[256,128]{1,0:T(8,128)} async-done(((f32[256,128]{1,0:T(8,128)}), f32[256,128]{1,0:T(8,128)}) %all-reduce.2.cloned.1.call-update) | async-done | bytes 131088 | tf_op jit(solution)/shard_map/while/body/eval_jaxpr/psum | solution.py:102
  1365.4 2.2 collective-permute-start
  1367.6 4.1 collective-permute-done
  1373.5 108.2 %all-reduce.2.cloned.1.call-done = f32[256,128]{1,0:T(8,128)} async-done(((f32[256,128]{1,0:T(8,128)}), f32[256,128]{1,0:T(8,128)}) %all-reduce.2.cloned.1.call-update) | async-done | bytes 131088 | tf_op jit(solution)/shard_map/while/body/eval_jaxpr/psum | solution.py:102
  1487.2 2.2 collective-permute-start
  1489.4 4.1 collective-permute-done
  1495.4 116.4 %all-reduce.2.cloned.1.call-done = f32[256,128]{1,0:T(8,128)} async-done(((f32[256,128]{1,0:T(8,128)}), f32[256,128]{1,0:T(8,128)}) %all-reduce.2.cloned.1.call-update) | async-done | bytes 131088 | tf_op jit(solution)/shard_map/while/body/eval_jaxpr/psum | solution.py:102
  1617.3 2.2 collective-permute-start
  1619.5 24.6 %collective-permute-done = f32[256,128]{0,1:T(8,128)S(1)} collective-permute-done((f32[256,128]{0,1:T(8,128)}, f32[256,128]{0,1:T(8,128)S(1)}, u32[]{:S(2)}, u32[]{:S(2)}) %collective-permute-start) | collective-permute-done | bytes 131104 | tf_op jit(solution)/shard_map/while/body/eval_jaxpr/ppermute | solution.py:10
  1644.2 5.8 conditional.6
  1644.2 3.6 fusion.8
  1647.8 2.2 fusion.14
  1650.7 83.5 %all-reduce.2.cloned.1.call-done = f32[256,128]{1,0:T(8,128)} async-done(((f32[256,128]{1,0:T(8,128)}), f32[256,128]{1,0:T(8,128)}) %all-reduce.2.cloned.1.call-update) | async-done | bytes 131088 | tf_op jit(solution)/shard_map/while/body/eval_jaxpr/psum | solution.py:102
  1734.2 30.6 %conditional.7 = (f32[256,128]{0,1:T(8,128)}, f32[1024,128]{0,1:T(8,128)}, f32[256,1024]{1,0:T(8,128)S(1)}) conditional(s32[]{:T(128)} %convert_element_type.52, f32[256,1024]{1,0:T(8,128)S(1)} %get-tuple-element.547, (f32[256,128]{1,0:T(8,128)}, f32[256,1024]{1,0:T(8,128)}) %tuple.78), branch_computations={%region_5.5_spmd, %region_6.8_spmd} | conditional | flops 906379392 | bytes 6030390 | solution.py:103
  1735.7 11.7 cholesky.2
  1748.7 9.8 custom-call.5
  1759.5 2.8 fusion.16
  1762.3 2.5 convolution_subtract_fusion
  1770.7 4.4 collective-permute-done
  1777.0 87.8 %all-reduce.2.cloned.1.call-done = f32[256,128]{1,0:T(8,128)} async-done(((f32[256,128]{1,0:T(8,128)}), f32[256,128]{1,0:T(8,128)}) %all-reduce.2.cloned.1.call-update) | async-done | bytes 131088 | tf_op jit(solution)/shard_map/while/body/eval_jaxpr/psum | solution.py:102
  1866.3 25.6 %collective-permute-start.1 = (f32[1024,128]{0,1:T(8,128)}, f32[1024,128]{0,1:T(8,128)S(1)}, u32[]{:S(2)}, u32[]{:S(2)}) collective-permute-start(f32[1024,128]{0,1:T(8,128)} %get-tuple-element.508), channel_id=1, source_target_pairs={{8,0},{16,8},{24,16},{32,24},{40,32},{48,40},{56,48},{9,1},{17,9},... | collective-permute-start | bytes 1572872 | tf_op jit(solution)/shard_map/while/body/eval_jaxpr/ppermute | solution.py:10
  1896.0 4.4 collective-permute-done
  1902.2 85.6 %all-reduce.2.cloned.1.call-done = f32[256,128]{1,0:T(8,128)} async-done(((f32[256,128]{1,0:T(8,128)}), f32[256,128]{1,0:T(8,128)}) %all-reduce.2.cloned.1.call-update) | async-done | bytes 131088 | tf_op jit(solution)/shard_map/while/body/eval_jaxpr/psum | solution.py:102
  1993.3 31.3 %collective-permute-start = (f32[256,128]{0,1:T(8,128)}, f32[256,128]{0,1:T(8,128)S(1)}, u32[]{:S(2)}, u32[]{:S(2)}) collective-permute-start(f32[256,128]{0,1:T(8,128)} %get-tuple-element.507), channel_id=1, source_target_pairs={{8,0},{16,8},{24,16},{32,24},{40,32},{48,40},{56,48},{9,1},{17,9},... | collective-permute-start | bytes 393224 | tf_op jit(solution)/shard_map/while/body/eval_jaxpr/ppermute | solution.py:10
  2024.7 2.8 collective-permute-done
  2027.5 55.2 %psum.21 = f32[1024]{0:T(1024)S(1)} all-reduce(f32[1024]{0:T(1024)S(1)} %get-tuple-element.342), channel_id=1, replica_groups=mesh['dp'=16,'section'=8,'tensor'=8] {'dp'}, use_global_device_ids=true, to_apply=%region_10.11 | all-reduce | flops 1024 | bytes 8192 | tf_op jit(solution)/shard_map/psum | solution.py:121
  (288 shorter events, 162.9 us)
Async XLA Ops:
  8.4 1.0 copy-start.2
  8.5 1.0 copy-start.4
  9.4 98.0 %all-reduce.2.cloned.1.call-start = ((), (), s32[]{:S(2)}) async-start(), calls=%async_computation | async-start | bytes 262144 | tf_op jit(solution)/shard_map/while/body/eval_jaxpr/psum | solution.py:102
  10.6 0.6 copy-start.3
  109.0 10.3 collective-permute-start.1
  113.0 6.3 collective-permute-start
  119.3 107.3 %all-reduce.2.cloned.1.call-start = ((), (), s32[]{:S(2)}) async-start(), calls=%async_computation | async-start | bytes 262144 | tf_op jit(solution)/shard_map/while/body/eval_jaxpr/psum | solution.py:102
  120.5 0.6 copy-start.3
  228.1 10.3 collective-permute-start.1
  232.1 6.3 collective-permute-start
  238.4 117.8 %all-reduce.2.cloned.1.call-start = ((), (), s32[]{:S(2)}) async-start(), calls=%async_computation | async-start | bytes 262144 | tf_op jit(solution)/shard_map/while/body/eval_jaxpr/psum | solution.py:102
  357.7 10.3 collective-permute-start.1
  361.7 6.3 collective-permute-start
  368.0 110.0 %all-reduce.2.cloned.1.call-start = ((), (), s32[]{:S(2)}) async-start(), calls=%async_computation | async-start | bytes 262144 | tf_op jit(solution)/shard_map/while/body/eval_jaxpr/psum | solution.py:102
  479.5 10.3 collective-permute-start.1
  483.5 6.3 collective-permute-start
  489.8 118.3 %all-reduce.2.cloned.1.call-start = ((), (), s32[]{:S(2)}) async-start(), calls=%async_computation | async-start | bytes 262144 | tf_op jit(solution)/shard_map/while/body/eval_jaxpr/psum | solution.py:102
  491.0 0.6 copy-start.3
  609.6 30.9 %collective-permute-start.1 = (f32[1024,128]{0,1:T(8,128)}, f32[1024,128]{0,1:T(8,128)S(1)}, u32[]{:S(2)}, u32[]{:S(2)}) collective-permute-start(f32[1024,128]{0,1:T(8,128)} %get-tuple-element.508), channel_id=1, source_target_pairs={{8,0},{16,8},{24,16},{32,24},{40,32},{48,40},{56,48},{9,1},{17,9},... | collective-permute-start | bytes 1572872 | tf_op jit(solution)/shard_map/while/body/eval_jaxpr/ppermute | solution.py:10
  613.6 26.9 %collective-permute-start = (f32[256,128]{0,1:T(8,128)}, f32[256,128]{0,1:T(8,128)S(1)}, u32[]{:S(2)}, u32[]{:S(2)}) collective-permute-start(f32[256,128]{0,1:T(8,128)} %get-tuple-element.507), channel_id=1, source_target_pairs={{8,0},{16,8},{24,16},{32,24},{40,32},{48,40},{56,48},{9,1},{17,9},... | collective-permute-start | bytes 393224 | tf_op jit(solution)/shard_map/while/body/eval_jaxpr/ppermute | solution.py:10
  640.5 90.0 %all-reduce.2.cloned.1.call-start = ((), (), s32[]{:S(2)}) async-start(), calls=%async_computation | async-start | bytes 262144 | tf_op jit(solution)/shard_map/while/body/eval_jaxpr/psum | solution.py:102
  646.3 0.6 copy-start.3
  732.0 22.9 %copy-start.1 = (f32[256,128]{1,0:T(8,128)S(1)}, f32[256,128]{1,0:T(8,128)}, u32[]{:S(2)}) copy-start(f32[256,128]{1,0:T(8,128)} %get-tuple-element.312) | copy-start | bytes 393220 | tf_op jit(solution)/shard_map/while/body/eval_jaxpr/cond
  761.1 10.3 collective-permute-start.1
  765.1 6.3 collective-permute-start
  771.5 89.7 %all-reduce.2.cloned.1.call-start = ((), (), s32[]{:S(2)}) async-start(), calls=%async_computation | async-start | bytes 262144 | tf_op jit(solution)/shard_map/while/body/eval_jaxpr/psum | solution.py:102
  772.6 0.6 copy-start.3
  862.6 34.0 %collective-permute-start.1 = (f32[1024,128]{0,1:T(8,128)}, f32[1024,128]{0,1:T(8,128)S(1)}, u32[]{:S(2)}, u32[]{:S(2)}) collective-permute-start(f32[1024,128]{0,1:T(8,128)} %get-tuple-element.508), channel_id=1, source_target_pairs={{8,0},{16,8},{24,16},{32,24},{40,32},{48,40},{56,48},{9,1},{17,9},... | collective-permute-start | bytes 1572872 | tf_op jit(solution)/shard_map/while/body/eval_jaxpr/ppermute | solution.py:10
  890.3 6.3 collective-permute-start
  896.6 87.8 %all-reduce.2.cloned.1.call-start = ((), (), s32[]{:S(2)}) async-start(), calls=%async_computation | async-start | bytes 262144 | tf_op jit(solution)/shard_map/while/body/eval_jaxpr/psum | solution.py:102
  897.8 0.6 copy-start.3
  986.0 38.2 %collective-permute-start.1 = (f32[1024,128]{0,1:T(8,128)}, f32[1024,128]{0,1:T(8,128)S(1)}, u32[]{:S(2)}, u32[]{:S(2)}) collective-permute-start(f32[1024,128]{0,1:T(8,128)} %get-tuple-element.508), channel_id=1, source_target_pairs={{8,0},{16,8},{24,16},{32,24},{40,32},{48,40},{56,48},{9,1},{17,9},... | collective-permute-start | bytes 1572872 | tf_op jit(solution)/shard_map/while/body/eval_jaxpr/ppermute | solution.py:10
  990.0 34.2 %collective-permute-start = (f32[256,128]{0,1:T(8,128)}, f32[256,128]{0,1:T(8,128)S(1)}, u32[]{:S(2)}, u32[]{:S(2)}) collective-permute-start(f32[256,128]{0,1:T(8,128)} %get-tuple-element.507), channel_id=1, source_target_pairs={{8,0},{16,8},{24,16},{32,24},{40,32},{48,40},{56,48},{9,1},{17,9},... | collective-permute-start | bytes 393224 | tf_op jit(solution)/shard_map/while/body/eval_jaxpr/ppermute | solution.py:10
  1024.1 87.1 %all-reduce.2.cloned.1.call-start = ((), (), s32[]{:S(2)}) async-start(), calls=%async_computation | async-start | bytes 262144 | tf_op jit(solution)/shard_map/while/body/eval_jaxpr/psum | solution.py:102
  1112.7 10.3 collective-permute-start.1
  1116.7 6.3 collective-permute-start
  1123.0 107.3 %all-reduce.2.cloned.1.call-start = ((), (), s32[]{:S(2)}) async-start(), calls=%async_computation | async-start | bytes 262144 | tf_op jit(solution)/shard_map/while/body/eval_jaxpr/psum | solution.py:102
  1231.8 10.3 collective-permute-start.1
  1235.8 6.3 collective-permute-start
  1242.1 117.8 %all-reduce.2.cloned.1.call-start = ((), (), s32[]{:S(2)}) async-start(), calls=%async_computation | async-start | bytes 262144 | tf_op jit(solution)/shard_map/while/body/eval_jaxpr/psum | solution.py:102
  1243.3 0.6 copy-start.3
  1361.4 10.3 collective-permute-start.1
  1365.4 6.3 collective-permute-start
  1371.7 110.0 %all-reduce.2.cloned.1.call-start = ((), (), s32[]{:S(2)}) async-start(), calls=%async_computation | async-start | bytes 262144 | tf_op jit(solution)/shard_map/while/body/eval_jaxpr/psum | solution.py:102
  1372.9 0.6 copy-start.3
  1483.2 10.3 collective-permute-start.1
  1487.2 6.3 collective-permute-start
  1493.5 118.3 %all-reduce.2.cloned.1.call-start = ((), (), s32[]{:S(2)}) async-start(), calls=%async_computation | async-start | bytes 262144 | tf_op jit(solution)/shard_map/while/body/eval_jaxpr/psum | solution.py:102
  1494.7 0.6 copy-start.3
  1613.3 30.9 %collective-permute-start.1 = (f32[1024,128]{0,1:T(8,128)}, f32[1024,128]{0,1:T(8,128)S(1)}, u32[]{:S(2)}, u32[]{:S(2)}) collective-permute-start(f32[1024,128]{0,1:T(8,128)} %get-tuple-element.508), channel_id=1, source_target_pairs={{8,0},{16,8},{24,16},{32,24},{40,32},{48,40},{56,48},{9,1},{17,9},... | collective-permute-start | bytes 1572872 | tf_op jit(solution)/shard_map/while/body/eval_jaxpr/ppermute | solution.py:10
  1617.3 26.9 %collective-permute-start = (f32[256,128]{0,1:T(8,128)}, f32[256,128]{0,1:T(8,128)S(1)}, u32[]{:S(2)}, u32[]{:S(2)}) collective-permute-start(f32[256,128]{0,1:T(8,128)} %get-tuple-element.507), channel_id=1, source_target_pairs={{8,0},{16,8},{24,16},{32,24},{40,32},{48,40},{56,48},{9,1},{17,9},... | collective-permute-start | bytes 393224 | tf_op jit(solution)/shard_map/while/body/eval_jaxpr/ppermute | solution.py:10
  1644.2 90.0 %all-reduce.2.cloned.1.call-start = ((), (), s32[]{:S(2)}) async-start(), calls=%async_computation | async-start | bytes 262144 | tf_op jit(solution)/shard_map/while/body/eval_jaxpr/psum | solution.py:102
  1650.0 0.6 copy-start.3
  1735.7 22.9 %copy-start.1 = (f32[256,128]{1,0:T(8,128)S(1)}, f32[256,128]{1,0:T(8,128)}, u32[]{:S(2)}) copy-start(f32[256,128]{1,0:T(8,128)} %get-tuple-element.312) | copy-start | bytes 393220 | tf_op jit(solution)/shard_map/while/body/eval_jaxpr/cond
  1764.8 10.3 collective-permute-start.1
  1768.8 6.3 collective-permute-start
  1775.1 89.7 %all-reduce.2.cloned.1.call-start = ((), (), s32[]{:S(2)}) async-start(), calls=%async_computation | async-start | bytes 262144 | tf_op jit(solution)/shard_map/while/body/eval_jaxpr/psum | solution.py:102
  1776.3 0.6 copy-start.3
  1866.3 34.0 %collective-permute-start.1 = (f32[1024,128]{0,1:T(8,128)}, f32[1024,128]{0,1:T(8,128)S(1)}, u32[]{:S(2)}, u32[]{:S(2)}) collective-permute-start(f32[1024,128]{0,1:T(8,128)} %get-tuple-element.508), channel_id=1, source_target_pairs={{8,0},{16,8},{24,16},{32,24},{40,32},{48,40},{56,48},{9,1},{17,9},... | collective-permute-start | bytes 1572872 | tf_op jit(solution)/shard_map/while/body/eval_jaxpr/ppermute | solution.py:10
  1894.0 6.3 collective-permute-start
  1900.3 87.5 %all-reduce.2.cloned.1.call-start = ((), (), s32[]{:S(2)}) async-start(), calls=%async_computation | async-start | bytes 262144 | tf_op jit(solution)/shard_map/while/body/eval_jaxpr/psum | solution.py:102
  1989.3 38.2 %collective-permute-start.1 = (f32[1024,128]{0,1:T(8,128)}, f32[1024,128]{0,1:T(8,128)S(1)}, u32[]{:S(2)}, u32[]{:S(2)}) collective-permute-start(f32[1024,128]{0,1:T(8,128)} %get-tuple-element.508), channel_id=1, source_target_pairs={{8,0},{16,8},{24,16},{32,24},{40,32},{48,40},{56,48},{9,1},{17,9},... | collective-permute-start | bytes 1572872 | tf_op jit(solution)/shard_map/while/body/eval_jaxpr/ppermute | solution.py:10
  1993.3 34.2 %collective-permute-start = (f32[256,128]{0,1:T(8,128)}, f32[256,128]{0,1:T(8,128)S(1)}, u32[]{:S(2)}, u32[]{:S(2)}) collective-permute-start(f32[256,128]{0,1:T(8,128)} %get-tuple-element.507), channel_id=1, source_target_pairs={{8,0},{16,8},{24,16},{32,24},{40,32},{48,40},{56,48},{9,1},{17,9},... | collective-permute-start | bytes 393224 | tf_op jit(solution)/shard_map/while/body/eval_jaxpr/ppermute | solution.py:10
  2027.5 55.8 %copy-start = (f32[256,1024]{1,0:T(8,128)}, f32[256,1024]{1,0:T(8,128)S(1)}, u32[]{:S(2)}) copy-start(f32[256,1024]{1,0:T(8,128)S(1)} %get-tuple-element.341) | copy-start | bytes 3145732
  (5 other events, 3.2 us)
Sparse Core Ops, SparseCore 0:
  12.6 94.8 all-reduce.1
  122.4 104.1 all-reduce.1
  241.5 114.6 all-reduce.1
  370.8 107.1 all-reduce.1
  492.6 115.4 all-reduce.1
  647.1 83.3 all-reduce.1
  774.6 86.4 all-reduce.1
  899.8 84.6 all-reduce.1
  1027.2 83.8 all-reduce.1
  1125.8 104.4 all-reduce.1
  1245.2 114.6 all-reduce.1
  1374.5 107.1 all-reduce.1
  1496.6 115.1 all-reduce.1
  1650.8 83.3 all-reduce.1
  1777.9 86.8 all-reduce.1
  1903.2 84.6 all-reduce.1
where the time goes:
time: 2090 us
  waiting for transfers between devices  1690 us (81%)
  starting transfers between devices  170 us (8%)
  local copies, waits for them, and re-layouts  66.8 us (3%)
  other arithmetic  62.4 us (3%)
  blocking collectives  55.2 us (3%)
  matrix products  26.8 us (1%)
    psum x16, waiting for transfers between devices, advance(): proj = lax.psum(partial_value, 'tensor')  1590 us
    ppermute x32, starting transfers between devices, shifted(): return lax.ppermute(array, axis, pairs)  170 us
    ppermute x32, waiting for transfers between devices, shifted(): return lax.ppermute(array, axis, pairs)  105 us
    psum x1, blocking collectives, body(): summed = lax.psum(gain_total, 'dp')  55.2 us
  transfers between devices with their start and end apart: 48, of which 32 were waited for; matrix products, arithmetic and copies ran while one was open for 2% of the time, Pallas kernels for 0%

commit v1 on v0

v1 whole, which is shorter than its diff:
```python
import jax
import jax.numpy as jnp
from jax import lax
from jax.sharding import PartitionSpec as P

HIGH = lax.Precision.HIGH
HIGHEST = lax.Precision.HIGHEST


def dot(left, right, over, precision):
    return lax.dot_general(
        left,
        right,
        (over, ((), ())),
        preferred_element_type=jnp.float32,
        precision=precision,
    )


def summed_over(array, axis):
    size = lax.axis_size(axis)
    rows, cols = array.shape
    chunks = lax.all_to_all(array.reshape(size, rows // size, cols), axis, 0, 0)
    mine = jnp.sum(chunks, axis=0)
    copies = jnp.broadcast_to(mine[None], (size, rows // size, cols))
    return lax.all_to_all(copies, axis, 0, 0).reshape(rows, cols)


def body(section_inputs, out_grad, layer_gain, init_factor):
    sections = lax.axis_size("section")
    section = lax.axis_index("section")
    micros = section_inputs.shape[1]
    rows = section_inputs.shape[2]
    width = section_inputs.shape[3]
    rank = init_factor.shape[2]
    basis = init_factor[0]
    is_last = section == sections - 1

    saved = section_inputs[0].astype(jnp.float32)
    soft = jnp.tanh(saved)
    weight = layer_gain * (1.0 + soft * soft)
    slope = 2.0 * saved - soft

    factor_m = jnp.zeros((rows, rank), jnp.float32)
    factor_q = jnp.zeros((width, rank), jnp.float32)
    residue = jnp.zeros((rows, width), jnp.float32)
    gain_total = jnp.zeros((width,), jnp.float32)
    sent = [jnp.zeros((rows, width), jnp.bfloat16) for _ in range(micros)]

    def pick(array, micro):
        return lax.dynamic_index_in_dim(array, micro, 0, keepdims=False)

    for stage in range(sections + micros - 1):
        micro = stage - (sections - 1 - section)
        active = (micro >= 0) & (micro < micros)
        micro = jnp.clip(micro, 0, micros - 1)
        upstream = dot(factor_m, factor_q, ((1,), (1,)), HIGH)
        if stage < micros:
            upstream = jnp.where(is_last, out_grad[stage].astype(jnp.float32), upstream)
        local = upstream * pick(weight, micro)
        merged = local + residue
        partial = dot(merged, basis, ((1,), (0,)), HIGH)
        proj = summed_over(partial, "tensor")
        gain_total += jnp.where(active, jnp.sum(upstream * pick(slope, micro), axis=0), 0.0)
        for m in range(micros):
            sent[m] = jnp.where(active & (micro == m), local.astype(jnp.bfloat16), sent[m])
        pairs = [
            (s, s - 1)
            for s in range(1, sections)
            if 0 <= stage - (sections - 1 - s) < micros
        ]
        out_q = dot(merged, proj, ((0,), (0,)), HIGH)
        if pairs:
            factor_q = lax.ppermute(out_q, "section", pairs)
        gram = dot(proj, proj, ((0,), (0,)), HIGHEST)
        lower = jnp.linalg.cholesky(gram)
        inverse = lax.linalg.triangular_solve(
            lower, jnp.eye(rank, dtype=jnp.float32), left_side=True, lower=True
        )
        ortho = dot(proj, inverse, ((1,), (1,)), HIGHEST)
        out_m = dot(ortho, inverse, ((1,), (0,)), HIGHEST)
        if pairs:
            factor_m = lax.ppermute(out_m, "section", pairs)
        residue = jnp.where(active, merged - dot(out_m, out_q, ((1,), (1,)), HIGH), residue)

    n_dp = lax.axis_size("dp")
    gathered = lax.all_to_all(
        jnp.broadcast_to(gain_total.reshape(1, 8, width // 8), (n_dp, 8, width // 8)), "dp", 0, 0
    )
    summed = jnp.sum(gathered, axis=0).reshape(width)
    gain_grad = summed * (1.0 / jnp.sqrt(jnp.float32(micros * rows * n_dp)))
    return (jnp.stack(sent)[None], residue[None], gain_grad[None])


def solution(mesh):
    placed = (
        P("section", None, "dp", "tensor"),
        P(None, "dp", "tensor"),
        P("section", "tensor"),
        P("section", "tensor", None),
    )
    return jax.shard_map(
        body,
        mesh=mesh,
        in_specs=placed,
        out_specs=(
            P("section", None, "dp", "tensor"),
            P("section", "dp", "tensor"),
            P("section", "tensor"),
        ),
        check_vma=False,
    )
```

time: 2090 us -> 613 us (0.29)
  the two profiles are of different devices: /device:TPU:176 before, /device:TPU:2 now
where the time goes in v1:
time: 613 us; the launch traced here: 603 us
  other arithmetic  221 us (36%)
  blocking collectives  191 us (31%)
  matrix products  83.7 us (14%)
  waiting for transfers between devices  47.9 us (8%)
  starting transfers between devices  45.2 us (7%)
  local copies, waits for them, and re-layouts  11.3 us (2%)
    another operation x27, other arithmetic, body(): lower = jnp.linalg.cholesky(gram)  111 us
    all_to_all x8, blocking collectives, summed_over(): chunks = lax.all_to_all(array.reshape(size, rows // size, cols), axis, 0, 0)  97.7 us
    another operation x18, other arithmetic, body(): lax.linalg.triangular_solve(lower, jnp.eye(rank, dtype=jnp.float32), left...  94.2 us
    all_to_all x8, blocking collectives, summed_over(): return lax.all_to_all(copies, axis, 0, 0).reshape(rows, cols)  93.2 us
    dot_general x63, matrix products, dot(): lax.dot_general(left, right, (over, ((), ())), preferred_element_type=jnp...  81.2 us
    ppermute x8, waiting for transfers between devices, body(): factor_m = lax.ppermute(out_m, 'section', pairs)  28.2 us
    all_to_all x1, starting transfers between devices, body(): lax.all_to_all(jnp.broadcast_to(gain_total.reshape(1, 8, width // 8), (n_...  16.9 us
    ppermute x8, starting transfers between devices, body(): factor_q = lax.ppermute(out_q, 'section', pairs)  12.9 us
  transfers between devices with their start and end apart: 19, of which 4 were waited for; matrix products, arithmetic and copies ran while one was open for 30% of the time, Pallas kernels for 0%

profile of v1, /device:TPU:2, one launch (start us, length us, event | category | flops | bytes accessed | tf_op | source)
XLA Modules:
  0.0 602.8 jit_solution(16456497922608454737)
XLA Ops:
  5.4 16.5 %all_to_all.95 = f32[8,32,128]{2,1,0:T(8,128)S(1)} all-to-all(f32[8,32,128]{2,1,0:T(8,128)S(1)} %fusion.40), channel_id=1, replica_groups=mesh['dp'=16,'section'=8,'tensor'=8] {'tensor'}, dimensions={0} | all-to-all | bytes 262144 | tf_op jit(solution)/shard_map/all_to_all | solution.py:23
  21.9 11.5 %all_to_all.96 = f32[8,32,128]{2,1,0:T(8,128)S(1)} all-to-all(f32[8,32,128]{2,1,0:T(8,128)S(1)} %broadcast_in_dim.45), channel_id=1, replica_groups=mesh['dp'=16,'section'=8,'tensor'=8] {'tensor'}, dimensions={0} | all-to-all | bytes 262144 | tf_op jit(solution)/shard_map/all_to_all | solution.py:26
  33.9 11.7 %cholesky.149 = f32[128,128]{1,0:T(8,128)S(1)} custom-call(f32[128,128]{1,0:T(8,128)S(1)} %fusion.103), custom_call_target="Cholesky" | custom-call | tf_op jit(solution)/shard_map/jit(cholesky)/cholesky | solution.py:76
  47.0 9.8 %custom-call.13 = f32[1,128,128]{1,2,0:T(8,128)S(1)} custom-call(f32[1,128,128]{2,1,0:T(8,128)S(1)} %fusion.77), custom_call_target="InvertDiagBlocksLowerTriangular" | custom-call | tf_op jit(solution)/shard_map/triangular_solve/custom-call.0 | solution.py:77
  57.1 2.2 fusion.116
  62.0 1.9 convolution_select_fusion
  63.9 1.8 fusion.43
  67.3 11.5 %all_to_all.97 = f32[8,32,128]{2,1,0:T(8,128)S(1)} all-to-all(f32[8,32,128]{2,1,0:T(8,128)S(1)} %fusion.38), channel_id=1, replica_groups=mesh['dp'=16,'section'=8,'tensor'=8] {'tensor'}, dimensions={0} | all-to-all | bytes 262144 | tf_op jit(solution)/shard_map/all_to_all | solution.py:23
  78.8 11.7 %all_to_all.98 = f32[8,32,128]{2,1,0:T(8,128)S(1)} all-to-all(f32[8,32,128]{2,1,0:T(8,128)S(1)} %broadcast_in_dim.47), channel_id=1, replica_groups=mesh['dp'=16,'section'=8,'tensor'=8] {'tensor'}, dimensions={0} | all-to-all | bytes 262144 | tf_op jit(solution)/shard_map/all_to_all | solution.py:26
  90.5 2.2 fusion.119
  94.7 11.7 %cholesky.160 = f32[128,128]{1,0:T(8,128)S(1)} custom-call(f32[128,128]{1,0:T(8,128)S(1)} %fusion.101), custom_call_target="Cholesky" | custom-call | tf_op jit(solution)/shard_map/jit(cholesky)/cholesky | solution.py:76
  107.8 9.8 %custom-call.14 = f32[1,128,128]{1,2,0:T(8,128)S(1)} custom-call(f32[1,128,128]{2,1,0:T(8,128)S(1)} %fusion.78), custom_call_target="InvertDiagBlocksLowerTriangular" | custom-call | tf_op jit(solution)/shard_map/triangular_solve/custom-call.0 | solution.py:77
  119.1 1.7 fusion.120
  120.9 3.4 fusion.45
  125.9 11.5 %all_to_all.99 = f32[8,32,128]{2,1,0:T(8,128)S(1)} all-to-all(f32[8,32,128]{2,1,0:T(8,128)S(1)} %fusion.36), channel_id=1, replica_groups=mesh['dp'=16,'section'=8,'tensor'=8] {'tensor'}, dimensions={0} | all-to-all | bytes 262144 | tf_op jit(solution)/shard_map/all_to_all | solution.py:23
  137.4 11.5 %all_to_all.100 = f32[8,32,128]{2,1,0:T(8,128)S(1)} all-to-all(f32[8,32,128]{2,1,0:T(8,128)S(1)} %broadcast_in_dim.48), channel_id=1, replica_groups=mesh['dp'=16,'section'=8,'tensor'=8] {'tensor'}, dimensions={0} | all-to-all | bytes 262144 | tf_op jit(solution)/shard_map/all_to_all | solution.py:26
  148.9 2.2 fusion.123
  151.1 1.8 collective-permute-start.5
  153.5 11.7 %cholesky.171 = f32[128,128]{1,0:T(8,128)S(1)} custom-call(f32[128,128]{1,0:T(8,128)S(1)} %fusion.99), custom_call_target="Cholesky" | custom-call | tf_op jit(solution)/shard_map/jit(cholesky)/cholesky | solution.py:76
  166.5 9.8 %custom-call.15 = f32[1,128,128]{1,2,0:T(8,128)S(1)} custom-call(f32[1,128,128]{2,1,0:T(8,128)S(1)} %fusion.79), custom_call_target="InvertDiagBlocksLowerTriangular" | custom-call | tf_op jit(solution)/shard_map/triangular_solve/custom-call.0 | solution.py:77
  179.6 3.5 fusion.47
  184.7 11.5 %all_to_all.101 = f32[8,32,128]{2,1,0:T(8,128)S(1)} all-to-all(f32[8,32,128]{2,1,0:T(8,128)S(1)} %fusion.34), channel_id=1, replica_groups=mesh['dp'=16,'section'=8,'tensor'=8] {'tensor'}, dimensions={0} | all-to-all | bytes 262144 | tf_op jit(solution)/shard_map/all_to_all | solution.py:23
  196.2 11.5 %all_to_all.102 = f32[8,32,128]{2,1,0:T(8,128)S(1)} all-to-all(f32[8,32,128]{2,1,0:T(8,128)S(1)} %broadcast_in_dim.49), channel_id=1, replica_groups=mesh['dp'=16,'section'=8,'tensor'=8] {'tensor'}, dimensions={0} | all-to-all | bytes 262144 | tf_op jit(solution)/shard_map/all_to_all | solution.py:26
  207.7 2.2 fusion.127
  212.1 11.7 %cholesky.182 = f32[128,128]{1,0:T(8,128)S(1)} custom-call(f32[128,128]{1,0:T(8,128)S(1)} %fusion.97), custom_call_target="Cholesky" | custom-call | tf_op jit(solution)/shard_map/jit(cholesky)/cholesky | solution.py:76
  225.1 9.8 %custom-call.16 = f32[1,128,128]{1,2,0:T(8,128)S(1)} custom-call(f32[1,128,128]{2,1,0:T(8,128)S(1)} %fusion.80), custom_call_target="InvertDiagBlocksLowerTriangular" | custom-call | tf_op jit(solution)/shard_map/triangular_solve/custom-call.0 | solution.py:77
  238.2 3.4 fusion.49
  243.3 12.6 %all_to_all.103 = f32[8,32,128]{2,1,0:T(8,128)S(1)} all-to-all(f32[8,32,128]{2,1,0:T(8,128)S(1)} %fusion.32), channel_id=1, replica_groups=mesh['dp'=16,'section'=8,'tensor'=8] {'tensor'}, dimensions={0} | all-to-all | bytes 262144 | tf_op jit(solution)/shard_map/all_to_all | solution.py:23
  255.9 11.5 %all_to_all.104 = f32[8,32,128]{2,1,0:T(8,128)S(1)} all-to-all(f32[8,32,128]{2,1,0:T(8,128)S(1)} %broadcast_in_dim.96), channel_id=1, replica_groups=mesh['dp'=16,'section'=8,'tensor'=8] {'tensor'}, dimensions={0} | all-to-all | bytes 262144 | tf_op jit(solution)/shard_map/all_to_all | solution.py:26
  267.3 2.2 fusion.131
  271.7 11.7 %cholesky.193 = f32[128,128]{1,0:T(8,128)S(1)} custom-call(f32[128,128]{1,0:T(8,128)S(1)} %fusion.95), custom_call_target="Cholesky" | custom-call | tf_op jit(solution)/shard_map/jit(cholesky)/cholesky | solution.py:76
  284.8 9.8 %custom-call.17 = f32[1,128,128]{1,2,0:T(8,128)S(1)} custom-call(f32[1,128,128]{2,1,0:T(8,128)S(1)} %fusion.81), custom_call_target="InvertDiagBlocksLowerTriangular" | custom-call | tf_op jit(solution)/shard_map/triangular_solve/custom-call.0 | solution.py:77
  297.9 3.5 fusion.51
  303.0 11.5 %all_to_all.105 = f32[8,32,128]{2,1,0:T(8,128)S(1)} all-to-all(f32[8,32,128]{2,1,0:T(8,128)S(1)} %fusion.30), channel_id=1, replica_groups=mesh['dp'=16,'section'=8,'tensor'=8] {'tensor'}, dimensions={0} | all-to-all | bytes 262144 | tf_op jit(solution)/shard_map/all_to_all | solution.py:23
  314.5 11.5 %all_to_all.106 = f32[8,32,128]{2,1,0:T(8,128)S(1)} all-to-all(f32[8,32,128]{2,1,0:T(8,128)S(1)} %broadcast_in_dim.97), channel_id=1, replica_groups=mesh['dp'=16,'section'=8,'tensor'=8] {'tensor'}, dimensions={0} | all-to-all | bytes 262144 | tf_op jit(solution)/shard_map/all_to_all | solution.py:26
  325.9 2.2 fusion.135
  328.2 1.8 collective-permute-start.11
  330.5 11.7 %cholesky.204 = f32[128,128]{1,0:T(8,128)S(1)} custom-call(f32[128,128]{1,0:T(8,128)S(1)} %fusion.93), custom_call_target="Cholesky" | custom-call | tf_op jit(solution)/shard_map/jit(cholesky)/cholesky | solution.py:76
  343.6 9.8 %custom-call.18 = f32[1,128,128]{1,2,0:T(8,128)S(1)} custom-call(f32[1,128,128]{2,1,0:T(8,128)S(1)} %fusion.82), custom_call_target="InvertDiagBlocksLowerTriangular" | custom-call | tf_op jit(solution)/shard_map/triangular_solve/custom-call.0 | solution.py:77
  356.7 3.4 fusion.53
  361.7 11.5 %all_to_all.107 = f32[8,32,128]{2,1,0:T(8,128)S(1)} all-to-all(f32[8,32,128]{2,1,0:T(8,128)S(1)} %fusion.28), channel_id=1, replica_groups=mesh['dp'=16,'section'=8,'tensor'=8] {'tensor'}, dimensions={0} | all-to-all | bytes 262144 | tf_op jit(solution)/shard_map/all_to_all | solution.py:23
  373.2 11.5 %all_to_all.108 = f32[8,32,128]{2,1,0:T(8,128)S(1)} all-to-all(f32[8,32,128]{2,1,0:T(8,128)S(1)} %broadcast_in_dim.98), channel_id=1, replica_groups=mesh['dp'=16,'section'=8,'tensor'=8] {'tensor'}, dimensions={0} | all-to-all | bytes 262144 | tf_op jit(solution)/shard_map/all_to_all | solution.py:26
  384.7 2.2 fusion.139
  388.9 11.7 %cholesky.215 = f32[128,128]{1,0:T(8,128)S(1)} custom-call(f32[128,128]{1,0:T(8,128)S(1)} %fusion.91), custom_call_target="Cholesky" | custom-call | tf_op jit(solution)/shard_map/jit(cholesky)/cholesky | solution.py:76
  402.0 9.8 %custom-call.19 = f32[1,128,128]{1,2,0:T(8,128)S(1)} custom-call(f32[1,128,128]{2,1,0:T(8,128)S(1)} %fusion.83), custom_call_target="InvertDiagBlocksLowerTriangular" | custom-call | tf_op jit(solution)/shard_map/triangular_solve/custom-call.0 | solution.py:77
  413.9 28.2 %collective-permute-done.12 = f32[256,128]{1,0:T(8,128)S(1)} collective-permute-done((f32[256,128]{1,0:T(8,128)S(1)}, f32[256,128]{1,0:T(8,128)S(1)}, u32[]{:S(2)}, u32[]{:S(2)}) %collective-permute-start.12) | collective-permute-done | bytes 131104 | tf_op jit(solution)/shard_map/ppermute | solution.py:83
  443.7 3.4 fusion.55
  448.7 11.4 %all_to_all.109 = f32[8,32,128]{2,1,0:T(8,128)S(1)} all-to-all(f32[8,32,128]{2,1,0:T(8,128)S(1)} %fusion.26), channel_id=1, replica_groups=mesh['dp'=16,'section'=8,'tensor'=8] {'tensor'}, dimensions={0} | all-to-all | bytes 262144 | tf_op jit(solution)/shard_map/all_to_all | solution.py:23
  460.1 12.8 %all_to_all.110 = f32[8,32,128]{2,1,0:T(8,128)S(1)} all-to-all(f32[8,32,128]{2,1,0:T(8,128)S(1)} %broadcast_in_dim.99), channel_id=1, replica_groups=mesh['dp'=16,'section'=8,'tensor'=8] {'tensor'}, dimensions={0} | all-to-all | bytes 262144 | tf_op jit(solution)/shard_map/all_to_all | solution.py:26
  472.9 2.2 fusion.143
  477.2 11.7 %cholesky.226 = f32[128,128]{1,0:T(8,128)S(1)} custom-call(f32[128,128]{1,0:T(8,128)S(1)} %fusion.89), custom_call_target="Cholesky" | custom-call | tf_op jit(solution)/shard_map/jit(cholesky)/cholesky | solution.py:76
  490.2 9.8 %custom-call.20 = f32[1,128,128]{1,2,0:T(8,128)S(1)} custom-call(f32[1,128,128]{2,1,0:T(8,128)S(1)} %fusion.84), custom_call_target="InvertDiagBlocksLowerTriangular" | custom-call | tf_op jit(solution)/shard_map/triangular_solve/custom-call.0 | solution.py:77
  502.2 2.9 fusion
  505.1 8.8 %fusion.23 = (f32[1024]{0:T(1024)S(1)}, f32[1024]{0:T(1024)S(1)}, f32[1024]{0:T(1024)S(1)}, f32[1024]{0:T(1024)S(1)}, f32[1024]{0:T(1024)S(1)}, /*index=5*/f32[1...) fusion(f32[256,1024]{1,0:T(8,128)} %get-tuple-element.24, ...), kind=kOutput, calls=%fused_computation.55 | convolution fusion | flops 206035968 | bytes 19566628 | tf_op jit(solution)/shard_map/dot_general | solution.py:11
  513.9 1.8 fusion.56
  518.0 3.6 all-to-all-start.16
  521.7 7.4 %select_bitcast_fusion.1 = (bf16[1,256,1024]{2,1,0:T(8,128)(2,1)S(1)}, bf16[256,1024]{1,0:T(8,128)(2,1)}, bf16[256,1024]{1,0:T(8,128)(2,1)}, bf16[256,1024]{1,0:...) fusion(pred[]{:T(512)S(6)} %and.99, ...), kind=kLoop, calls=%fused_computation.84 | loop fusion | flops 6815744 | bytes 22544424 | tf_op jit(solution)/shard_map/stack | solution.py:92
  529.1 2.0 all-to-all-done.16
  531.8 16.9 %all-to-all-start.18 = ((f32[16,8,128]{2,1,0:T(8,128)}), f32[16,8,128]{2,1,0:T(8,128)S(1)}, u32[]{:S(2)}, u32[]{:S(2)}) async-start(f32[16,8,128]{2,1,0:T(8,128)} %broadcast_in_dim.104), calls=%async_computation.18 | async-start | bytes 131072 | tf_op jit(solution)/shard_map/all_to_all | solution.py:87
  550.3 9.9 %all-to-all-done.18 = f32[16,8,128]{2,1,0:T(8,128)S(1)} async-done(((f32[16,8,128]{2,1,0:T(8,128)}), f32[16,8,128]{2,1,0:T(8,128)S(1)}, u32[]{:S(2)}, u32[]{:S(2)}) %all-to-all-start.18) | async-done | bytes 65568 | tf_op jit(solution)/shard_map/all_to_all | solution.py:87
  560.9 5.3 all-to-all-start.17
  567.9 7.7 %all-to-all-done.17 = f32[8,32,128]{2,1,0:T(8,128)S(1)} async-done(((f32[8,32,128]{2,1,0:T(8,128)}), f32[8,32,128]{2,1,0:T(8,128)S(1)}, u32[]{:S(2)}, u32[]{:S(2)}) %all-to-all-start.17) | async-done | bytes 131104 | tf_op jit(solution)/shard_map/all_to_all | solution.py:26
  577.1 11.7 %cholesky.237 = f32[128,128]{1,0:T(8,128)S(1)} custom-call(f32[128,128]{1,0:T(8,128)S(1)} %fusion.87), custom_call_target="Cholesky" | custom-call | tf_op jit(solution)/shard_map/jit(cholesky)/cholesky | solution.py:76
  590.1 9.8 %custom-call.21 = f32[1,128,128]{1,2,0:T(8,128)S(1)} custom-call(f32[1,128,128]{2,1,0:T(8,128)S(1)} %fusion.85), custom_call_target="InvertDiagBlocksLowerTriangular" | custom-call | tf_op jit(solution)/shard_map/triangular_solve/custom-call.0 | solution.py:77
  (212 shorter events, 73.7 us)
Async XLA Ops:
  0.6 4.2 copy-start
  0.7 1.7 copy-start.29
  3.9 1.0 copy-start.1
  59.3 2.7 collective-permute-start.1
  61.3 0.7 collective-permute-start
  62.0 1.9 copy-start.2
  63.9 1.8 copy-start.5
  65.8 1.0 copy-start.3
  92.7 26.4 %collective-permute-start.3 = (f32[1024,128]{1,0:T(8,128)S(1)}, f32[1024,128]{1,0:T(8,128)}, u32[]{:S(2)}, u32[]{:S(2)}) collective-permute-start(f32[1024,128]{1,0:T(8,128)S(1)} %fusion.119), channel_id=1, source_target_pairs={{48,40},{56,48},{49,41},{57,49},{50,42},{58,50},{51,43},{59,51},{5... | collective-permute-start | bytes 1572872 | tf_op jit(solution)/shard_map/ppermute | solution.py:74
  118.4 0.7 collective-permute-start.2
  119.1 1.8 copy-start.4
  120.9 3.4 copy-start.20
  124.3 1.0 copy-start.10
  151.1 26.8 %collective-permute-start.5 = (f32[1024,128]{1,0:T(8,128)S(1)}, f32[1024,128]{1,0:T(8,128)}, u32[]{:S(2)}, u32[]{:S(2)}) collective-permute-start(f32[1024,128]{1,0:T(8,128)S(1)} %fusion.123), channel_id=1, source_target_pairs={{40,32},{48,40},{41,33},{49,41},{42,34},{50,42},{43,35},{51,43},{4... | collective-permute-start | bytes 1572872 | tf_op jit(solution)/shard_map/ppermute | solution.py:74
  177.2 0.7 collective-permute-start.4
  177.9 1.8 copy-start.11
  179.6 3.5 copy-start.21
  183.1 1.0 copy-start.12
  209.9 26.6 %collective-permute-start.7 = (f32[1024,128]{1,0:T(8,128)S(1)}, f32[1024,128]{1,0:T(8,128)}, u32[]{:S(2)}, u32[]{:S(2)}) collective-permute-start(f32[1024,128]{1,0:T(8,128)S(1)} %fusion.127), channel_id=1, source_target_pairs={{32,24},{40,32},{33,25},{41,33},{34,26},{42,34},{35,27},{43,35},{3... | collective-permute-start | bytes 1572872 | tf_op jit(solution)/shard_map/ppermute | solution.py:74
  235.8 0.7 collective-permute-start.6
  236.5 1.8 copy-start.13
  238.2 3.4 copy-start.22
  241.6 1.0 copy-start.14
  269.6 26.6 %collective-permute-start.9 = (f32[1024,128]{1,0:T(8,128)S(1)}, f32[1024,128]{1,0:T(8,128)}, u32[]{:S(2)}, u32[]{:S(2)}) collective-permute-start(f32[1024,128]{1,0:T(8,128)S(1)} %fusion.131), channel_id=1, source_target_pairs={{24,16},{32,24},{25,17},{33,25},{26,18},{34,26},{27,19},{35,27},{2... | collective-permute-start | bytes 1572872 | tf_op jit(solution)/shard_map/ppermute | solution.py:74
  295.5 0.7 collective-permute-start.8
  296.1 1.8 copy-start.15
  297.9 3.5 copy-start.23
  301.4 1.0 copy-start.16
  328.2 26.8 %collective-permute-start.11 = (f32[1024,128]{1,0:T(8,128)S(1)}, f32[1024,128]{1,0:T(8,128)}, u32[]{:S(2)}, u32[]{:S(2)}) collective-permute-start(f32[1024,128]{1,0:T(8,128)S(1)} %fusion.135), channel_id=1, source_target_pairs={{16,8},{24,16},{17,9},{25,17},{18,10},{26,18},{19,11},{27,19},{20,... | collective-permute-start | bytes 1572872 | tf_op jit(solution)/shard_map/ppermute | solution.py:74
  354.2 0.7 collective-permute-start.10
  354.9 1.8 copy-start.17
  356.7 3.4 copy-start.24
  360.1 1.0 copy-start.18
  386.9 55.2 %collective-permute-start.13 = (f32[1024,128]{1,0:T(8,128)S(1)}, f32[1024,128]{1,0:T(8,128)}, u32[]{:S(2)}, u32[]{:S(2)}) collective-permute-start(f32[1024,128]{1,0:T(8,128)S(1)} %fusion.139), channel_id=1, source_target_pairs={{8,0},{16,8},{9,1},{17,9},{10,2},{18,10},{11,3},{19,11},{12,4},{20... | collective-permute-start | bytes 1572872 | tf_op jit(solution)/shard_map/ppermute | solution.py:74
  412.6 29.5 %collective-permute-start.12 = (f32[256,128]{1,0:T(8,128)S(1)}, f32[256,128]{1,0:T(8,128)S(1)}, u32[]{:S(2)}, u32[]{:S(2)}) collective-permute-start(f32[256,128]{1,0:T(8,128)S(1)} %fusion.138), channel_id=1, source_target_pairs={{8,0},{16,8},{9,1},{17,9},{10,2},{18,10},{11,3},{19,11},{12,4},{20... | collective-permute-start | bytes 393224 | tf_op jit(solution)/shard_map/ppermute | solution.py:83
  413.9 29.8 %copy-start.19 = (f32[256,1024]{1,0:T(8,128)S(1)}, f32[256,1024]{1,0:T(8,128)}, u32[]{:S(2)}) copy-start(f32[256,1024]{1,0:T(8,128)} %copy-done.18) | copy-start | bytes 3145732
  443.7 3.4 copy-start.25
  447.2 1.0 copy-start.8
  475.1 29.9 %collective-permute-start.15 = (f32[1024,128]{1,0:T(8,128)S(1)}, f32[1024,128]{1,0:T(8,128)}, u32[]{:S(2)}, u32[]{:S(2)}) collective-permute-start(f32[1024,128]{1,0:T(8,128)S(1)} %fusion.143), channel_id=1, source_target_pairs={{8,0},{9,1},{10,2},{11,3},{12,4},{13,5},{14,6},{15,7},{72,64},{73,... | collective-permute-start | bytes 1572872 | tf_op jit(solution)/shard_map/ppermute | solution.py:74
  500.9 4.2 collective-permute-start.14
  505.1 8.9 %copy-start.9 = (f32[256,1024]{1,0:T(8,128)S(1)}, f32[256,1024]{1,0:T(8,128)}, u32[]{:S(2)}) copy-start(f32[256,1024]{1,0:T(8,128)} %copy-done.8) | copy-start | bytes 3145732
  505.1 8.9 %copy-start.28 = (f32[256,1024]{1,0:T(8,128)S(1)}, f32[256,1024]{1,0:T(8,128)}, u32[]{:S(2)}) copy-start(f32[256,1024]{1,0:T(8,128)} %get-tuple-element.38) | copy-start | bytes 3145732
  513.9 1.9 copy-start.26
  515.8 1.0 copy-start.6
  518.0 13.1 %all-to-all-start.16 = ((f32[8,32,128]{2,1,0:T(8,128)}), f32[8,32,128]{2,1,0:T(8,128)S(1)}, u32[]{:S(2)}, u32[]{:S(2)}) async-start(f32[8,32,128]{2,1,0:T(8,128)} %fusion.24), calls=%async_computation.16 | async-start | bytes 262144 | tf_op jit(solution)/shard_map/all_to_all | solution.py:23
  531.8 28.5 %all-to-all-start.18 = ((f32[16,8,128]{2,1,0:T(8,128)}), f32[16,8,128]{2,1,0:T(8,128)S(1)}, u32[]{:S(2)}, u32[]{:S(2)}) async-start(f32[16,8,128]{2,1,0:T(8,128)} %broadcast_in_dim.104), calls=%async_computation.18 | async-start | bytes 131072 | tf_op jit(solution)/shard_map/all_to_all | solution.py:87
  550.3 25.3 %copy-start.7 = (f32[256,1024]{1,0:T(8,128)S(1)}, f32[256,1024]{1,0:T(8,128)}, u32[]{:S(2)}) copy-start(f32[256,1024]{1,0:T(8,128)} %copy-done.6) | copy-start | bytes 3145732
  560.9 14.7 %all-to-all-start.17 = ((f32[8,32,128]{2,1,0:T(8,128)}), f32[8,32,128]{2,1,0:T(8,128)S(1)}, u32[]{:S(2)}, u32[]{:S(2)}) async-start(f32[8,32,128]{2,1,0:T(8,128)} %broadcast_in_dim.101), calls=%async_computation.17 | async-start | bytes 262144 | tf_op jit(solution)/shard_map/all_to_all | solution.py:26
  567.3 33.6 %copy-start.27 = (f32[256,1024]{1,0:T(8,128)S(1)}, f32[256,1024]{1,0:T(8,128)}, u32[]{:S(2)}) copy-start(f32[256,1024]{1,0:T(8,128)} %get-tuple-element.40) | copy-start | bytes 3145732
